TPU v7x, 256 devices: a whole 4x4x8 slice. The times are simulated.
256 devices in a mesh: scene: 32 (over z, x), seq: 8 (over y, core).
Axes of the slice: x: 4, y: 4, z: 8, core: 2. Of those that a mesh axis runs over, the one named last changes fastest.
Arguments:
- x_in: bfloat16 [262144, 256], P(('scene', 'seq')), may hold values from -6 to 6
- counts: int32 [32], P('scene'), may hold values from 1024 to 8192, as said below
- ln_gains: float32 [2, 256], replicated, may hold values from 0.5 to 1.5
- w_qkv: bfloat16 [2, 256, 768], replicated
- w_proj: bfloat16 [2, 256, 256], replicated, may hold values from -0.375 to 0.375
- cotangent: bfloat16 [262144, 256], P(('scene', 'seq')), may hold values from -24 to 24
Outputs:
- result_out: bfloat16 [262144, 256], P(('scene', 'seq'))
- grad_input: bfloat16 [262144, 256], P(('scene', 'seq'))
- grad_gains: float32 [2, 256], replicated
- grad_qkv: float32 [2, 256, 768], replicated
- grad_proj: float32 [2, 256, 256], replicated
Inputs may be any that keep to these rules, and one draw needn't show every extreme that they name: `counts`: some scene has all 8192 slots occupied.
All inputs are finite; a program needn't handle non-finite values.
Results may differ from a plain program's by a relative error of at most 0.034.
Values may be sent and summed in bfloat16 or wider, within the bound.
No kernel may reach another device: no remote copies, remote signals or barrier semaphores. Data moves between devices by JAX's collectives and lax.ppermute only.
A program may use at most 128 MiB of HBM per device.

v0:
```python
import functools

import jax
import jax.numpy as jnp
from jax import lax
from jax.experimental import pallas as pl
from jax.experimental.pallas import tpu as pltpu
from jax.sharding import PartitionSpec as P

HEADS = 8
WIN = 1024
C = 256
HALF = 128
SPLIT = 8
PIECE = WIN // SPLIT
EPSILON = 1e-05
BLOCKED = -1e30
SCALE = (C // HEADS) ** (-0.5)
LOG2E = 1.4426950408889634
LN2 = 0.6931471805599453
f32 = jnp.float32
bf16 = jnp.bfloat16
NN = (((1,), (0,)), ((), ()))
NT = (((1,), (1,)), ((), ()))
TN = (((0,), (0,)), ((), ()))
dot = functools.partial(lax.dot_general, preferred_element_type=f32)
LIMIT = 56 * 2**20


def lanes():
    lane = lax.broadcasted_iota(jnp.int32, (1, HALF), 1)
    return lane >> 5, lane & 31


def norm_parts(x):
    average = jnp.mean(x, axis=-1, keepdims=True)
    centred = x - average
    spread = jnp.mean(centred * centred, axis=-1, keepdims=True)
    rstd = lax.rsqrt(spread + EPSILON)
    return centred * rstd, rstd


def project(normed, wq_ref, qkv_ref):
    packed = dot(normed, wq_ref[...], NN)
    for part in range(6):
        piece = packed[:, part * HALF : (part + 1) * HALF]
        if part < 2:
            piece = piece * (SCALE * LOG2E)
        qkv_ref[part] = piece.astype(bf16)


def group_extras(valid):
    _, l32 = lanes()
    vq = jnp.where(valid, 1.0, 0.0).astype(f32)
    for_q = jnp.where(l32 == 0, vq, jnp.where(l32 == 1, 1.0 - vq, 0.0)).astype(bf16)
    for_k = jnp.where(l32 == 0, BLOCKED * (1.0 - vq), jnp.where(l32 == 1, BLOCKED * vq, 0.0)).astype(bf16)
    return for_q, for_k


def head_masks(j):
    blk, _ = lanes()
    own = blk == j
    nxt = blk == ((j + 1) & 3)
    return own, nxt, own.astype(f32).astype(bf16), nxt.astype(f32).astype(bf16)


def attend_heads(heads, q, k, v, for_q, for_k, e_ref, vv_ref):
    for i, j in enumerate(heads):
        _, _, own_b, nxt_b = head_masks(j)
        q_aug = q * own_b + for_q * nxt_b
        k_aug = k * (1 - nxt_b) + for_k * nxt_b
        scores = dot(q_aug, k_aug, NT)
        largest = jnp.max(scores, axis=1, keepdims=True)
        e_ref[:, i * WIN : (i + 1) * WIN] = jnp.exp2(scores - largest).astype(bf16)
        vv_ref[i * WIN : (i + 1) * WIN, :HALF] = v * own_b
        vv_ref[i * WIN : (i + 1) * WIN, HALF:] = jnp.broadcast_to(own_b, (WIN, HALF))
    return dot(e_ref[...], vv_ref[...], NN)


def delta_parts(d_mixed, mixed, sums):
    blk_r = lax.broadcasted_iota(jnp.int32, (HALF, HALF), 0) >> 5
    blk_c = lax.broadcasted_iota(jnp.int32, (HALF, HALF), 1) >> 5
    same = (blk_c == blk_r).astype(f32).astype(bf16)
    _, l32 = lanes()
    product = d_mixed * mixed
    high = product.astype(bf16)
    low = (product - high.astype(f32)).astype(bf16)
    over = 1.0 / sums
    delta = pltpu.roll(-(dot(high, same, NN) + dot(low, same, NN)) * over, 32, 1)
    high = delta.astype(bf16).astype(f32)
    extra = jnp.where(l32 == 0, high, jnp.where(l32 == 1, delta - high, 0.0)).astype(bf16)
    return d_mixed * over, extra


def attend_back_heads(heads, e_ref, q_t, k, v, d_own, d_own_t, extra, ds_ref, kk_ref, dk_ref, dv_ref, base):
    for i, j in enumerate(heads):
        _, _, own_b, nxt_b = head_masks(j)
        e = e_ref[:, i * WIN : (i + 1) * WIN]
        d_weights = dot(d_own * own_b + extra * nxt_b, v * own_b + (1 - own_b), NT)
        d_scores = e * d_weights.astype(bf16)
        kk_ref[i * WIN : (i + 1) * WIN, :] = k * own_b
        rows = slice(i * 32, (i + 1) * 32)
        dst = pl.ds(pl.multiple_of(base + i * 32, 32), 32)
        dv_ref[dst, :] = dot(d_own_t[rows], e, NN).astype(bf16)
        ds_ref[:, i * WIN : (i + 1) * WIN] = d_scores
        dk_ref[dst, :] = (dot(q_t[rows], d_scores, NN) * LN2).astype(bf16)
    return dot(ds_ref[...], kk_ref[...], NN) * SCALE


def block_finish(x, gain, wq_ref, dq_ref, dk_ref, dv_ref, dy, put):
    xhat, rstd = norm_parts(x)
    normed = (xhat * gain).astype(bf16)
    d_normed = jnp.zeros((WIN, C), f32)
    for g in range(2):
        cols = slice(g * HALF, (g + 1) * HALF)
        put(g * HALF, dot(normed, dq_ref[g], TN))
        d_normed = d_normed + dot(dq_ref[g], wq_ref[:, cols], NT)
    for part, ref in ((1, dk_ref), (2, dv_ref)):
        put(part * C, dot(ref[...], normed, NN).T)
        w_t = wq_ref[:, part * C : (part + 1) * C].astype(f32).T.astype(bf16)
        d_normed = d_normed + dot(ref[...], w_t, TN)
    d_gain = jnp.sum(d_normed * xhat, axis=0, keepdims=True)
    d_hat = d_normed * gain
    mean_d = jnp.mean(d_hat, axis=-1, keepdims=True)
    mean_dx = jnp.mean(d_hat * xhat, axis=-1, keepdims=True)
    return dy.astype(f32) + rstd * (d_hat - mean_d - xhat * mean_dx), jnp.broadcast_to(d_gain, (HALF, C)).T


def near_valid(n):
    i = lax.broadcasted_iota(jnp.int32, (WIN, 1), 0)
    return ((i & (PIECE - 1)) * SPLIT + (i >> 7)) < n


def split_into(tmp, read, write):
    for g in range(2):
        tmp[g] = read(slice(g * HALF, (g + 1) * HALF))
    for g in range(2):
        for f in range(SPLIT):
            write(f, slice(g * HALF, (g + 1) * HALF), tmp[g, pl.ds(f, PIECE, stride=SPLIT), :].astype(bf16))


def merge_into(tmp, read, out_ref):
    for g in range(2):
        for f in range(SPLIT):
            tmp[g, pl.ds(f, PIECE, stride=SPLIT), :] = read(slice(f * PIECE, (f + 1) * PIECE), slice(g * HALF, (g + 1) * HALF))
    for g in range(2):
        out_ref[:, g * HALF : (g + 1) * HALF] = tmp[g].astype(bf16)


def near_forward_kernel(
    n_ref, x_ref, cot_ref, gain_ref, wq_ref, wo_ref, out_ref, xp_ref, qkv_ref, mixed_ref, sums_ref, e_ref, tmp, acc, vv, exq, exk
):
    step = pl.program_id(0)

    @pl.when(step == 0)
    def _():
        def put_x(f, cols, piece):
            xp_ref[f * PIECE : (f + 1) * PIECE, cols] = piece

        split_into(tmp, lambda cols: x_ref[:, cols].astype(f32), put_x)
        xhat, _ = norm_parts(xp_ref[...].astype(f32))
        project((xhat * gain_ref[0:1, :]).astype(bf16), wq_ref, qkv_ref)
        exq[...], exk[...] = group_extras(near_valid(n_ref[0]))

        def put_cot(f, cols, piece):
            out_ref[f * PIECE : (f + 1) * PIECE, C + cols.start : C + cols.stop] = piece

        kept = lax.broadcasted_iota(jnp.int32, (WIN, 1), 0) < n_ref[0]
        split_into(tmp, lambda cols: jnp.where(kept, cot_ref[:, cols].astype(f32), 0.0), put_cot)

    g = step >> 1
    first = (step & 1) * 2
    both = attend_heads(
        (first, first + 1), qkv_ref[g], qkv_ref[2 + g], qkv_ref[4 + g], exq[...], exk[...], e_ref, vv
    )

    @pl.when(first == 0)
    def _():
        acc[g] = both

    @pl.when(first != 0)
    def _():
        acc[g] = acc[g] + both

    @pl.when(step == 3)
    def _():
        y = xp_ref[...].astype(f32)
        for g in range(2):
            sums = acc[g, :, HALF:]
            sums_ref[g] = sums
            mixed = (acc[g, :, :HALF] / sums).astype(bf16)
            mixed_ref[g] = mixed
            y = y + dot(mixed, wo_ref[g * HALF : (g + 1) * HALF, :], NN)
        out_ref[:, :C] = y.astype(bf16)


def far_kernel(
    n_ref, in_ref, gain_ref, wq_ref, wo_ref, out_ref, pay_ref, qkv, dmix, mixed_s, dq, dk, dv, e_s, vv, kk, exq, exk
):
    g = pl.program_id(0)

    def valid():
        return lax.broadcasted_iota(jnp.int32, (WIN, 1), 0) < n_ref[0]

    @pl.when(g == 0)
    def _():
        xhat, _ = norm_parts(in_ref[:, :C].astype(f32))
        project((xhat * gain_ref[1:2, :]).astype(bf16), wq_ref, qkv)
        exq[...], exk[...] = group_extras(valid())
        d_mixed = dot(in_ref[:, C:], wo_ref[...], NT).astype(bf16)
        for i in range(2):
            dmix[i] = d_mixed[:, i * HALF : (i + 1) * HALF]

    q, k, v = qkv[g], qkv[2 + g], qkv[4 + g]
    both = attend_heads(range(4), q, k, v, exq[...], exk[...], e_s, vv)
    sums = both[:, HALF:]
    mixed = both[:, :HALF] / sums
    mixed_s[g] = mixed.astype(bf16)
    d_own, extra = delta_parts(dmix[g].astype(f32), mixed, sums)
    d_q = attend_back_heads(
        range(4), e_s, q.astype(f32).T.astype(bf16), k, v, d_own.astype(bf16), d_own.T.astype(bf16), extra, e_s, kk, dk, dv, g * HALF
    )
    dq[g] = d_q.astype(bf16)

    @pl.when(g == 1)
    def _():
        dy = in_ref[:, C:]
        x = in_ref[:, :C].astype(f32)
        y = x
        for i in range(2):
            y = y + dot(mixed_s[i], wo_ref[i * HALF : (i + 1) * HALF, :], NN)
            pay_ref[i * HALF : (i + 1) * HALF, 768:1024] = dot(mixed_s[i], dy, TN).astype(bf16)
        out_ref[:, C:] = jnp.where(valid(), y, 0.0).astype(bf16)

        def put(col, piece):
            pay_ref[:, col : col + piece.shape[1]] = piece.astype(bf16)

        dx, d_gain = block_finish(x, gain_ref[1:2, :], wq_ref, dq, dk, dv, dy, put)
        out_ref[:, :C] = dx.astype(bf16)
        put(1024, d_gain)


def near_backward_kernel(
    core_ref,
    in_ref,
    xp_ref,
    gain_ref,
    wq_ref,
    wo_ref,
    qkv_ref,
    mixed_ref,
    sums_ref,
    two_ref,
    e_ref,
    dx_ref,
    res_ref,
    keep_ref,
    send_ref,
    pay_ref,
    down,
    down_t,
    q_t,
    extra_s,
    dq,
    dk,
    dv,
    ds,
    kk,
    acc,
    tmp,
):
    step = pl.program_id(0)

    def put(col, piece):
        pay_ref[:, col : col + piece.shape[1]] = piece.astype(bf16)

    @pl.when(step == 0)
    def _():
        dy = in_ref[:, :C]
        d_mixed = dot(dy, wo_ref[...], NT).astype(bf16).astype(f32)
        for i in range(2):
            rows = slice(i * HALF, (i + 1) * HALF)
            d_own, extra = delta_parts(d_mixed[:, rows], mixed_ref[i].astype(f32), sums_ref[i])
            down[i] = d_own.astype(bf16)
            down_t[rows, :] = d_own.T.astype(bf16)
            q_t[rows, :] = qkv_ref[i].astype(f32).T.astype(bf16)
            extra_s[i] = extra
            pay_ref[rows, 768:1024] = dot(mixed_ref[i], dy, TN).astype(bf16)
        pay_ref[:, 1024:2048] = two_ref[:, :1024]
        merge_into(tmp, lambda rows, cols: in_ref[rows, C + cols.start : C + cols.stop].astype(f32), res_ref)

    g = step >> 1
    first = (step & 1) * 2
    base = pl.multiple_of(step * 64, 64)
    d_q = attend_back_heads(
        (first, first + 1),
        e_ref,
        q_t[pl.ds(base, 64), :],
        qkv_ref[2 + g],
        qkv_ref[4 + g],
        down[g],
        down_t[pl.ds(base, 64), :],
        extra_s[g],
        ds,
        kk,
        dk,
        dv,
        base,
    )

    @pl.when(first == 0)
    def _():
        acc[...] = d_q

    @pl.when(first != 0)
    def _():
        dq[g] = (acc[...] + d_q).astype(bf16)

    @pl.when(step == 3)
    def _():
        dx, d_gain = block_finish(
            xp_ref[...].astype(f32), gain_ref[0:1, :], wq_ref, dq, dk, dv, in_ref[:, :C], put
        )
        lane = lax.broadcasted_iota(jnp.int32, (1, HALF), 1)
        put(2048, jnp.where(lane == 0, d_gain, two_ref[:, 1024:1152].astype(f32)))
        merge_into(tmp, lambda rows, cols: dx[rows, cols], dx_ref)
        core = core_ref[0]
        keep_ref[...] = pay_ref[pl.ds(pl.multiple_of(core * HALF, HALF), HALF), :]
        send_ref[...] = pay_ref[pl.ds(pl.multiple_of((1 - core) * HALF, HALF), HALF), :]


def spread_kernel(core_ref, mine_ref, other_ref, gains_ref, qkv_ref, proj_ref, tmp):
    core = core_ref[0]
    for ref, half in ((mine_ref, core), (other_ref, 1 - core)):
        rows = pl.ds(pl.multiple_of(half * HALF, HALF), HALF)
        for b in range(2):
            qkv_ref[b, rows, :] = ref[:, b * 1024 : b * 1024 + 768].astype(f32)
            proj_ref[b, rows, :] = ref[:, b * 1024 + 768 : (b + 1) * 1024].astype(f32)
        tmp[rows, :] = ref[:, 2048:2176].astype(f32)
    gains_ref[...] = tmp[...].T[:2]


def layer(shape, which):
    return pl.BlockSpec((None,) + shape, lambda i: (which, 0, 0))


def spec(shape):
    return pl.BlockSpec(shape, lambda i: (0,) * len(shape))


SCALAR = pl.BlockSpec(memory_space=pltpu.SMEM)
HEAD_PAIR = pl.BlockSpec((WIN, 2 * WIN), lambda i: (0, i))
PARAMS = pltpu.CompilerParams(vmem_limit_bytes=LIMIT)
ROWS = (WIN, C)
PAIR_ROWS = (WIN, 2 * C)
SPLIT_ROWS = (2, WIN, HALF)


def sds(shape, dtype):
    return jax.ShapeDtypeStruct(shape, dtype)


def cost(products):
    return pl.CostEstimate(flops=products * HEADS * 2 * WIN * WIN * HALF, bytes_accessed=2**24, transcendentals=2**23)


def near_forward(n, x, cot, gain, wq, wo):
    return pl.pallas_call(
        near_forward_kernel,
        grid=(4,),
        in_specs=[SCALAR, spec(ROWS), spec(ROWS), spec((2, C)), layer((C, 3 * C), 0), layer((C, C), 0)],
        out_specs=[spec(PAIR_ROWS), spec(ROWS), spec((6, WIN, HALF)), spec(SPLIT_ROWS), spec(SPLIT_ROWS), HEAD_PAIR],
        out_shape=[
            sds(PAIR_ROWS, bf16),
            sds(ROWS, bf16),
            sds((6, WIN, HALF), bf16),
            sds(SPLIT_ROWS, bf16),
            sds(SPLIT_ROWS, f32),
            sds((WIN, HEADS * WIN), bf16),
        ],
        scratch_shapes=[
            pltpu.VMEM(SPLIT_ROWS, f32),
            pltpu.VMEM((2, WIN, C), f32),
            pltpu.VMEM((2 * WIN, C), bf16),
            pltpu.VMEM((WIN, HALF), bf16),
            pltpu.VMEM((WIN, HALF), bf16),
        ],
        compiler_params=PARAMS,
        cost_estimate=cost(2),
        name="near_forward",
    )(n, x, cot, gain, wq, wo)


def far_both(n, rows, gain, wq, wo):
    return pl.pallas_call(
        far_kernel,
        grid=(2,),
        in_specs=[SCALAR, spec(PAIR_ROWS), spec((2, C)), layer((C, 3 * C), 1), layer((C, C), 1)],
        out_specs=[spec(PAIR_ROWS), spec((C, 1152))],
        out_shape=[sds(PAIR_ROWS, bf16), sds((C, 1152), bf16)],
        scratch_shapes=[
            pltpu.VMEM((6, WIN, HALF), bf16),
            pltpu.VMEM(SPLIT_ROWS, bf16),
            pltpu.VMEM(SPLIT_ROWS, bf16),
            pltpu.VMEM(SPLIT_ROWS, bf16),
            pltpu.VMEM((C, WIN), bf16),
            pltpu.VMEM((C, WIN), bf16),
            pltpu.VMEM((WIN, 4 * WIN), bf16),
            pltpu.VMEM((4 * WIN, C), bf16),
            pltpu.VMEM((4 * WIN, HALF), bf16),
            pltpu.VMEM((WIN, HALF), bf16),
            pltpu.VMEM((WIN, HALF), bf16),
        ],
        compiler_params=PARAMS,
        cost_estimate=cost(6),
        name="far_both",
    )(n, rows, gain, wq, wo)


def near_backward(core, rows, xp, gain, wq, wo, qkv, mixed, sums, two, e):
    return pl.pallas_call(
        near_backward_kernel,
        grid=(4,),
        in_specs=[
            SCALAR,
            spec(PAIR_ROWS),
            spec(ROWS),
            spec((2, C)),
            layer((C, 3 * C), 0),
            layer((C, C), 0),
            spec((6, WIN, HALF)),
            spec(SPLIT_ROWS),
            spec(SPLIT_ROWS),
            spec((C, 1152)),
            HEAD_PAIR,
        ],
        out_specs=[spec(ROWS), spec(ROWS), spec((HALF, 2176)), spec((HALF, 2176))],
        out_shape=[sds(ROWS, bf16), sds(ROWS, bf16), sds((HALF, 2176), bf16), sds((HALF, 2176), bf16)],
        scratch_shapes=[
            pltpu.VMEM((C, 2176), bf16),
            pltpu.VMEM(SPLIT_ROWS, bf16),
            pltpu.VMEM((C, WIN), bf16),
            pltpu.VMEM((C, WIN), bf16),
            pltpu.VMEM(SPLIT_ROWS, bf16),
            pltpu.VMEM(SPLIT_ROWS, bf16),
            pltpu.VMEM((C, WIN), bf16),
            pltpu.VMEM((C, WIN), bf16),
            pltpu.VMEM((WIN, 2 * WIN), bf16),
            pltpu.VMEM((2 * WIN, HALF), bf16),
            pltpu.VMEM((WIN, HALF), f32),
            pltpu.VMEM(SPLIT_ROWS, f32),
        ],
        compiler_params=PARAMS,
        cost_estimate=cost(4),
        name="near_backward",
    )(core, rows, xp, gain, wq, wo, qkv, mixed, sums, two, e)


def spread(core, mine, other):
    vmem = pl.BlockSpec(memory_space=pltpu.VMEM)
    return pl.pallas_call(
        spread_kernel,
        in_specs=[SCALAR, vmem, vmem],
        out_shape=[sds((2, C), f32), sds((2, C, 3 * C), f32), sds((2, C, C), f32)],
        scratch_shapes=[pltpu.VMEM((C, HALF), f32)],
        compiler_params=PARAMS,
        name="spread",
    )(core, mine, other)


def exchange(rows, axis, groups=None):
    return lax.all_to_all(rows, axis, split_axis=0, concat_axis=0, tiled=True, axis_index_groups=groups)


def sum_everywhere(keep, send, factor):
    scenes, groups = lax.axis_size("scene"), lax.axis_size("seq")
    width = keep.shape[1]
    pair = [(i, i ^ 1) for i in range(groups)]
    chips = [list(range(core, groups, 2)) for core in range(2)]
    many = groups // 2
    part = (keep.astype(f32) + lax.ppermute(send, "seq", pair).astype(f32)).astype(bf16)
    part = jnp.sum(exchange(part.reshape(many, scenes, width), "seq", chips).astype(f32), axis=0)
    part = exchange(part.astype(bf16).reshape(scenes, 1, width), "scene").astype(f32)
    row = (jnp.sum(part, axis=0, keepdims=True) * factor).astype(bf16)
    rows = exchange(jnp.broadcast_to(row, (scenes, 1, width)), "scene").reshape(1, scenes, width)
    mine = exchange(jnp.broadcast_to(rows, (many, scenes, width)), "seq", chips).reshape(HALF, width)
    return mine, lax.ppermute(mine, "seq", pair)


def body(x_in, counts, ln_gains, w_qkv, w_proj, cotangent):
    groups = lax.axis_size("seq")
    place = lax.axis_index("seq")
    factor = (WIN * lax.axis_size("scene") * groups) ** (-0.5)
    n_near = counts - place * WIN
    n_far = (counts - place + groups - 1) // groups

    def swap(rows):
        return exchange(rows.reshape(SPLIT, PIECE, 2 * C), "seq").reshape(PAIR_ROWS)

    first, xp, qkv, mixed, sums, e = near_forward(n_near, x_in, cotangent, ln_gains, w_qkv, w_proj)
    back, pay_two = far_both(n_far, swap(first), ln_gains, w_qkv, w_proj)
    core = jnp.full((1,), place % 2, jnp.int32)
    d_input, result, keep, send = near_backward(
        core, swap(back), xp, ln_gains, w_qkv, w_proj, qkv, mixed, sums, pay_two, e
    )
    gains, grads, projs = spread(core, *sum_everywhere(keep, send, factor))
    return result, d_input, gains, grads, projs


def solution(mesh):
    in_specs = (P(("scene", "seq"), None), P("scene"), P(), P(), P(), P(("scene", "seq"), None))
    out_specs = (P(("scene", "seq"), None), P(("scene", "seq"), None), P(), P(), P())
    return jax.shard_map(body, mesh=mesh, in_specs=in_specs, out_specs=out_specs, check_vma=False)
```

profile of v0, /device:TPU:1, one launch (start us, length us, event | category | flops | bytes accessed | tf_op | source)
XLA Modules:
  0.0 207.7 jit_solution(9370174636847230446)
XLA Ops:
  1.3 23.4 %near_forward.1 = (bf16[1024,512]{1,0:T(8,128)(2,1)}, bf16[1024,256]{1,0:T(8,128)(2,1)}, bf16[6,1024,128]{2,1,0:T(8,128)(2,1)}, bf16[2,1024,128]{2,1,0:T(8,128)(...) custom-call(s32[1]{0:T(128)S(6)} %sub.24.n_ref, bf16[1024,256]{1,0:T(8,128)(2,1)} %x_ref.1, ...), custom_call_target="tpu_custom_call" | custom-call | flops 4294967296 | bytes 16777216 | tf_op jit(solution)/shard_map/near_forward/pallas_call | solution.py:368
  24.6 6.7 %all-to-all-start = ((bf16[8,128,512]{2,1,0:T(8,128)(2,1)}), bf16[8,128,512]{2,1,0:T(8,128)(2,1)S(1)}, u32[]{:S(2)}, u32[]{:S(2)}) async-start(bf16[8,128,512]{2,1,0:T(8,128)(2,1)} %bitcast.16), calls=%async_computation | async-start | bytes 2097152 | tf_op jit(solution)/shard_map/all_to_all | solution.py:472
  31.3 15.1 %all-to-all-done = bf16[8,128,512]{2,1,0:T(8,128)(2,1)S(1)} async-done(((bf16[8,128,512]{2,1,0:T(8,128)(2,1)}), bf16[8,128,512]{2,1,0:T(8,128)(2,1)S(1)}, u32[]{:S(2)}, u32[]{:S(2)}) %all-to-all-start) | async-done | bytes 1048608 | tf_op jit(solution)/shard_map/all_to_all | solution.py:472
  46.4 0.0 copy-start.1
  46.5 1.0 copy-done.1
  47.4 39.2 %far_both.1 = (bf16[1024,512]{1,0:T(8,128)(2,1)}, bf16[256,1152]{1,0:T(8,128)(2,1)}) custom-call(s32[1]{0:T(128)S(6)} %select_n.13.n_ref, bf16[1024,512]{1,0:T(8,128)(2,1)} %bitcast.17, f32[2,256]{1,0:T(2,128)} %gain_ref.5, bf16[2,256,768]{2,1,0:T(8,128)(2,1)} %wq_ref.5, bf16[2,256,256]{2,1,0:T(8,128)(2,1)} %wo_ref.5), custom_call_target="tpu_custom_call" | custom-call | flops 12884901888 | bytes 16777216 | tf_op jit(solution)/shard_map/far_both/pallas_call | solution.py:395
  86.6 4.3 %all-to-all-start.1 = ((bf16[8,128,512]{2,1,0:T(8,128)(2,1)}), bf16[8,128,512]{2,1,0:T(8,128)(2,1)S(1)}, u32[]{:S(2)}, u32[]{:S(2)}) async-start(bf16[8,128,512]{2,1,0:T(8,128)(2,1)} %bitcast.19), calls=%async_computation.1 | async-start | bytes 2097152 | tf_op jit(solution)/shard_map/all_to_all | solution.py:472
  90.9 15.1 %all-to-all-done.1 = bf16[8,128,512]{2,1,0:T(8,128)(2,1)S(1)} async-done(((bf16[8,128,512]{2,1,0:T(8,128)(2,1)}), bf16[8,128,512]{2,1,0:T(8,128)(2,1)S(1)}, u32[]{:S(2)}, u32[]{:S(2)}) %all-to-all-start.1) | async-done | bytes 1048608 | tf_op jit(solution)/shard_map/all_to_all | solution.py:472
  106.1 0.0 copy-start.2
  106.1 1.0 copy-done.2
  107.1 29.1 %near_backward.1 = (bf16[1024,256]{1,0:T(8,128)(2,1)}, bf16[1024,256]{1,0:T(8,128)(2,1)}, bf16[128,2176]{1,0:T(8,128)(2,1)}, bf16[128,2176]{1,0:T(8,128)(2,1)}) custom-call(s32[1]{0:T(128)} %bitcast.core_ref, bf16[1024,512]{1,0:T(8,128)(2,1)} %bitcast.18, bf16[1024,256]{1,0:T(8,128)(2,1)} %get-tuple-element.22.xp_ref, f32[2,256]{1,0:T(2,128)} %gain_ref.5, ...), custom_call_target="tpu_custom_call" | custom-call | flops 8589934592 | bytes 16777216 | tf_op jit(solution)/shard_map/near_backward/pallas_call | solution.py:421
  136.1 0.9 collective-permute-start
  137.0 1.8 collective-permute-done
  138.8 1.2 add_convert_fusion
  140.0 11.8 %all_to_all.30 = bf16[4,32,2176]{2,1,0:T(8,128)(2,1)S(1)} all-to-all(bf16[4,32,2176]{2,1,0:T(8,128)(2,1)S(1)} %bitcast.13), channel_id=1, replica_groups={{0,2,4,6},{1,3,5,7},{8,10,12,14},{9,11,13,15},{16,18,20,22},{17,19,21,2..., dimensions={0} | all-to-all | bytes 1114112 | tf_op jit(solution)/shard_map/all_to_all | solution.py:472
  151.8 0.1 reduce_sum.21
  151.9 0.5 broadcast.11
  152.4 0.7 reduce.2
  153.1 0.2 reshape.55
  153.2 19.6 %all_to_all.31 = bf16[32,2,1088]{2,1,0:T(2,128)(2,1)S(1)} all-to-all(bf16[32,2,1088]{2,1,0:T(2,128)(2,1)S(1)} %reshape.55), channel_id=1, replica_groups=mesh['scene'=32,'seq'=8] {'scene'}, dimensions={0} | all-to-all | bytes 278528 | tf_op jit(solution)/shard_map/all_to_all | solution.py:472
  172.8 0.1 reshape.56
  173.0 0.3 convert_reduce_fusion
  173.3 0.1 broadcast_in_dim.17
  173.4 1.4 reduce.3
  174.8 0.2 reshape.57
  175.0 12.8 %all_to_all.32 = bf16[32,2,1088]{2,1,0:T(2,128)(2,1)S(1)} all-to-all(bf16[32,2,1088]{2,1,0:T(2,128)(2,1)S(1)} %reshape.57), channel_id=1, replica_groups=mesh['scene'=32,'seq'=8] {'scene'}, dimensions={0} | all-to-all | bytes 278528 | tf_op jit(solution)/shard_map/all_to_all | solution.py:472
  187.8 0.1 reshape.58
  188.1 9.5 %all_to_all.33 = bf16[4,32,2176]{2,1,0:T(8,128)(2,1)S(1)} all-to-all(bf16[4,32,2176]{2,1,0:T(8,128)(2,1)S(1)} %broadcast_in_dim.19), channel_id=1, replica_groups={{0,2,4,6},{1,3,5,7},{8,10,12,14},{9,11,13,15},{16,18,20,22},{17,19,21,2..., dimensions={0} | all-to-all | bytes 1114112 | tf_op jit(solution)/shard_map/all_to_all | solution.py:472
  197.6 0.0 copy-start
  197.6 5.1 %collective-permute-start.1 = (bf16[128,2176]{1,0:T(8,128)(2,1)S(1)}, bf16[128,2176]{1,0:T(8,128)(2,1)S(1)}, u32[]{:S(2)}, u32[]{:S(2)}) collective-permute-start(bf16[128,2176]{1,0:T(8,128)(2,1)S(1)} %bitcast.14), channel_id=1, source_target_pairs={{0,1},{1,0},{2,3},{3,2},{4,5},{5,4},{6,7},{7,6},{8,9},{9,8},{10,11... | collective-permute-start | bytes 1671176 | tf_op jit(solution)/shard_map/ppermute | solution.py:487
  202.7 1.6 collective-permute-done.1.other_ref
  204.2 0.0 copy-done
  204.2 0.0 copy-start.3
  204.3 0.8 copy-done.3
  205.1 2.6 %spread.1 = (f32[2,256]{1,0:T(2,128)}, f32[2,256,768]{2,1,0:T(8,128)}, f32[2,256,256]{2,1,0:T(8,128)}) custom-call(s32[1]{0:T(128)} %bitcast.core_ref, bf16[128,2176]{1,0:T(8,128)(2,1)} %bitcast.15, bf16[128,2176]{1,0:T(8,128)(2,1)} %copy-done.3), custom_call_target="tpu_custom_call" | custom-call | tf_op jit(solution)/shard_map/spread/pallas_call | solution.py:461
  (3 shorter events, 0.1 us)
Async XLA Ops:
  24.6 21.8 %all-to-all-start = ((bf16[8,128,512]{2,1,0:T(8,128)(2,1)}), bf16[8,128,512]{2,1,0:T(8,128)(2,1)S(1)}, u32[]{:S(2)}, u32[]{:S(2)}) async-start(bf16[8,128,512]{2,1,0:T(8,128)(2,1)} %bitcast.16), calls=%async_computation | async-start | bytes 2097152 | tf_op jit(solution)/shard_map/all_to_all | solution.py:472
  46.4 1.0 copy-start.1
  86.6 19.4 %all-to-all-start.1 = ((bf16[8,128,512]{2,1,0:T(8,128)(2,1)}), bf16[8,128,512]{2,1,0:T(8,128)(2,1)S(1)}, u32[]{:S(2)}, u32[]{:S(2)}) async-start(bf16[8,128,512]{2,1,0:T(8,128)(2,1)} %bitcast.19), calls=%async_computation.1 | async-start | bytes 2097152 | tf_op jit(solution)/shard_map/all_to_all | solution.py:472
  106.1 1.0 copy-start.2
  136.1 2.7 %collective-permute-start = (bf16[128,2176]{1,0:T(8,128)(2,1)}, bf16[128,2176]{1,0:T(8,128)(2,1)S(1)}, u32[]{:S(2)}, u32[]{:S(2)}) collective-permute-start(bf16[128,2176]{1,0:T(8,128)(2,1)} %get-tuple-element.31), channel_id=1, source_target_pairs={{0,1},{1,0},{2,3},{3,2},{4,5},{5,4},{6,7},{7,6},{8,9},{9,8},{10,11... | collective-permute-start | bytes 1671176 | tf_op jit(solution)/shard_map/ppermute | solution.py:481
  197.6 6.7 %copy-start = (bf16[4,32,2176]{2,1,0:T(8,128)(2,1)}, bf16[4,32,2176]{2,1,0:T(8,128)(2,1)S(1)}, u32[]{:S(2)}) copy-start(bf16[4,32,2176]{2,1,0:T(8,128)(2,1)S(1)} %all_to_all.33) | copy-start | bytes 1671172
  197.6 6.7 %collective-permute-start.1 = (bf16[128,2176]{1,0:T(8,128)(2,1)S(1)}, bf16[128,2176]{1,0:T(8,128)(2,1)S(1)}, u32[]{:S(2)}, u32[]{:S(2)}) collective-permute-start(bf16[128,2176]{1,0:T(8,128)(2,1)S(1)} %bitcast.14), channel_id=1, source_target_pairs={{0,1},{1,0},{2,3},{3,2},{4,5},{5,4},{6,7},{7,6},{8,9},{9,8},{10,11... | collective-permute-start | bytes 1671176 | tf_op jit(solution)/shard_map/ppermute | solution.py:487
  204.2 0.8 copy-start.3
where the time goes:
time: 208 us
  Pallas kernels  94.2 us (45%)
  blocking collectives  53.7 us (26%)
  waiting for transfers between devices  33.6 us (16%)
  starting transfers between devices  17 us (8%)
  local copies, waits for them, and re-layouts  4.15 us (2%)
  other arithmetic  3.65 us (2%)
    all_to_all x4, blocking collectives, exchange(): lax.all_to_all(rows, axis, split_axis=0, concat_axis=0, tiled=True, axis_...  53.7 us
    pallas_call x1, Pallas kernels, far_both(): pl.pallas_call(far_kernel, grid=(2,), in_specs=[SCALAR, spec(PAIR_ROWS),...  39.2 us
    all_to_all x2, waiting for transfers between devices, exchange(): lax.all_to_all(rows, axis, split_axis=0, concat_axis=0, tiled=True, axis_...  30.2 us
    pallas_call x1, Pallas kernels, near_backward(): pl.pallas_call(near_backward_kernel, grid=(4,), in_specs=[SCALAR, spec(PA...  29.1 us
    pallas_call x1, Pallas kernels, near_forward(): pl.pallas_call(near_forward_kernel, grid=(4,), in_specs=[SCALAR, spec(ROW...  23.4 us
    all_to_all x2, starting transfers between devices, exchange(): lax.all_to_all(rows, axis, split_axis=0, concat_axis=0, tiled=True, axis_...  11 us
    ppermute x1, starting transfers between devices, sum_everywhere(): return (mine, lax.ppermute(mine, 'seq', pair))  5.11 us
  transfers between devices with their start and end apart: 4, of which 4 were waited for; matrix products, arithmetic and copies ran while one was open for 0% of the time, Pallas kernels for 0%

commit v1 on v0

v1 whole, which is shorter than its diff:
```python
import functools

import jax
import jax.numpy as jnp
from jax import lax
from jax.experimental import pallas as pl
from jax.experimental.pallas import tpu as pltpu
from jax.sharding import PartitionSpec as P

HEADS = 8
WIN = 1024
C = 256
HALF = 128
SPLIT = 8
PIECE = WIN // SPLIT
EPSILON = 1e-05
BLOCKED = -1e30
SCALE = (C // HEADS) ** (-0.5)
LOG2E = 1.4426950408889634
LN2 = 0.6931471805599453
f32 = jnp.float32
bf16 = jnp.bfloat16
NN = (((1,), (0,)), ((), ()))
NT = (((1,), (1,)), ((), ()))
TN = (((0,), (0,)), ((), ()))
dot = functools.partial(lax.dot_general, preferred_element_type=f32)
LIMIT = 56 * 2**20


def lanes():
    lane = lax.broadcasted_iota(jnp.int32, (1, HALF), 1)
    return lane >> 5, lane & 31


def norm_parts(x):
    average = jnp.mean(x, axis=-1, keepdims=True)
    centred = x - average
    spread = jnp.mean(centred * centred, axis=-1, keepdims=True)
    rstd = lax.rsqrt(spread + EPSILON)
    return centred * rstd, rstd


def project(normed, wq_ref, qkv_ref):
    packed = dot(normed, wq_ref[...], NN)
    for part in range(6):
        piece = packed[:, part * HALF : (part + 1) * HALF]
        if part < 2:
            piece = piece * (SCALE * LOG2E)
        qkv_ref[part] = piece.astype(bf16)


def group_extras(valid):
    _, l32 = lanes()
    vq = jnp.where(valid, 1.0, 0.0).astype(f32)
    for_q = jnp.where(l32 == 0, vq, jnp.where(l32 == 1, 1.0 - vq, 0.0)).astype(bf16)
    for_k = jnp.where(l32 == 0, BLOCKED * (1.0 - vq), jnp.where(l32 == 1, BLOCKED * vq, 0.0)).astype(bf16)
    return for_q, for_k


def head_masks(j):
    blk, _ = lanes()
    own = blk == j
    nxt = blk == ((j + 1) & 3)
    return own, nxt, own.astype(f32).astype(bf16), nxt.astype(f32).astype(bf16)


def attend_heads(heads, q, k, v, for_q, for_k, e_ref):
    total = sums = 0.0
    for i, j in enumerate(heads):
        own, nxt, own_b, nxt_b = head_masks(j)
        q_aug = q * own_b + for_q * nxt_b
        k_aug = k * (1 - nxt_b) + for_k * nxt_b
        scores = dot(q_aug, k_aug, NT)
        largest = jnp.max(scores, axis=1, keepdims=True)
        e = jnp.exp2(scores - largest).astype(bf16)
        e_ref[:, i * WIN : (i + 1) * WIN] = e
        both = dot(e, v * own_b + (1 - own_b), NN)
        total = total + jnp.where(own, both, 0.0)
        sums = sums + jnp.where(nxt, both, 0.0)
    return total, pltpu.roll(sums, 96, 1)


def delta_parts(d_mixed, mixed, sums):
    blk_r = lax.broadcasted_iota(jnp.int32, (HALF, HALF), 0) >> 5
    blk_c = lax.broadcasted_iota(jnp.int32, (HALF, HALF), 1) >> 5
    same = (blk_c == blk_r).astype(f32).astype(bf16)
    _, l32 = lanes()
    product = d_mixed * mixed
    high = product.astype(bf16)
    low = (product - high.astype(f32)).astype(bf16)
    over = 1.0 / sums
    delta = pltpu.roll(-(dot(high, same, NN) + dot(low, same, NN)) * over, 32, 1)
    high = delta.astype(bf16).astype(f32)
    extra = jnp.where(l32 == 0, high, jnp.where(l32 == 1, delta - high, 0.0)).astype(bf16)
    return d_mixed * over, extra


def attend_back_heads(heads, e_ref, q_t, k, v, d_own, d_own_t, extra, dk_ref, dv_ref, base):
    d_q = 0.0
    for i, j in enumerate(heads):
        _, _, own_b, nxt_b = head_masks(j)
        e = e_ref[:, i * WIN : (i + 1) * WIN]
        d_weights = dot(d_own * own_b + extra * nxt_b, v * own_b + (1 - own_b), NT)
        d_scores = e * d_weights.astype(bf16)
        rows = slice(i * 32, (i + 1) * 32)
        dst = pl.ds(pl.multiple_of(base + i * 32, 32), 32)
        dv_ref[dst, :] = dot(d_own_t[rows], e, NN).astype(bf16)
        dk_ref[dst, :] = (dot(q_t[rows], d_scores, NN) * LN2).astype(bf16)
        d_q = d_q + dot(d_scores, k * own_b, NN)
    return d_q * SCALE


def weight_grads(normed, dq_ref, dk_ref, dv_ref, put):
    for g in range(2):
        put(g * HALF, dot(normed, dq_ref[g], TN))
    put(C, dot(dk_ref[...], normed, NN).T)
    put(2 * C, dot(dv_ref[...], normed, NN).T)


def input_grad(x, gain, wq_ref, dq_ref, dk_ref, dv_ref, dy):
    xhat, rstd = norm_parts(x)
    d_normed = jnp.zeros((WIN, C), f32)
    for g in range(2):
        d_normed = d_normed + dot(dq_ref[g], wq_ref[:, g * HALF : (g + 1) * HALF], NT)
    for part, ref in ((1, dk_ref), (2, dv_ref)):
        w_t = wq_ref[:, part * C : (part + 1) * C].astype(f32).T.astype(bf16)
        d_normed = d_normed + dot(ref[...], w_t, TN)
    d_hat = d_normed * gain
    mean_d = jnp.mean(d_hat, axis=-1, keepdims=True)
    mean_dx = jnp.mean(d_hat * xhat, axis=-1, keepdims=True)
    return dy.astype(f32) + rstd * (d_hat - mean_d - xhat * mean_dx)


def near_valid(n):
    i = lax.broadcasted_iota(jnp.int32, (WIN, 1), 0)
    return ((i & (PIECE - 1)) * SPLIT + (i >> 7)) < n


def split_into(tmp, read, write):
    for g in range(2):
        tmp[g] = read(slice(g * HALF, (g + 1) * HALF))
    for g in range(2):
        for f in range(SPLIT):
            write(f, slice(g * HALF, (g + 1) * HALF), tmp[g, pl.ds(f, PIECE, stride=SPLIT), :].astype(bf16))


def merge_into(tmp, read, out_ref):
    for g in range(2):
        for f in range(SPLIT):
            tmp[g, pl.ds(f, PIECE, stride=SPLIT), :] = read(slice(f * PIECE, (f + 1) * PIECE), slice(g * HALF, (g + 1) * HALF))
    for g in range(2):
        out_ref[:, g * HALF : (g + 1) * HALF] = tmp[g].astype(bf16)


def near_forward_kernel(
    n_ref, x_ref, cot_ref, gain_ref, wq_ref, wo_ref, out_ref, xp_ref, normed_ref, qkv_ref, mixed_ref, sums_ref, e_ref, tmp, acc, exq, exk
):
    step = pl.program_id(0)

    @pl.when(step == 0)
    def _():
        def put_x(f, cols, piece):
            xp_ref[f * PIECE : (f + 1) * PIECE, cols] = piece

        split_into(tmp, lambda cols: x_ref[:, cols].astype(f32), put_x)
        xhat, _ = norm_parts(xp_ref[...].astype(f32))
        normed_ref[...] = (xhat * gain_ref[0:1, :]).astype(bf16)
        project(normed_ref[...], wq_ref, qkv_ref)
        exq[...], exk[...] = group_extras(near_valid(n_ref[0]))

        def put_cot(f, cols, piece):
            out_ref[f * PIECE : (f + 1) * PIECE, C + cols.start : C + cols.stop] = piece

        kept = lax.broadcasted_iota(jnp.int32, (WIN, 1), 0) < n_ref[0]
        split_into(tmp, lambda cols: jnp.where(kept, cot_ref[:, cols].astype(f32), 0.0), put_cot)

    g = step >> 1
    first = (step & 1) * 2
    total, sums = attend_heads(
        (first, first + 1), qkv_ref[g], qkv_ref[2 + g], qkv_ref[4 + g], exq[...], exk[...], e_ref
    )

    @pl.when(first == 0)
    def _():
        acc[g, :, :HALF] = total
        acc[g, :, HALF:] = sums

    @pl.when(first != 0)
    def _():
        acc[g, :, :HALF] = acc[g, :, :HALF] + total
        acc[g, :, HALF:] = acc[g, :, HALF:] + sums

    @pl.when(step == 3)
    def _():
        y = xp_ref[...].astype(f32)
        for g in range(2):
            sums = acc[g, :, HALF:]
            sums_ref[g] = sums
            mixed = (acc[g, :, :HALF] / sums).astype(bf16)
            mixed_ref[g] = mixed
            y = y + dot(mixed, wo_ref[g * HALF : (g + 1) * HALF, :], NN)
        out_ref[:, :C] = y.astype(bf16)


def far_kernel(
    n_ref, in_ref, gain_ref, wq_ref, wo_ref, out_ref, mixed_s, dq, dk, dv, qkv, dmix, e_s, exq, exk
):
    g = pl.program_id(0)

    def valid():
        return lax.broadcasted_iota(jnp.int32, (WIN, 1), 0) < n_ref[0]

    @pl.when(g == 0)
    def _():
        xhat, _ = norm_parts(in_ref[:, :C].astype(f32))
        project((xhat * gain_ref[1:2, :]).astype(bf16), wq_ref, qkv)
        exq[...], exk[...] = group_extras(valid())
        d_mixed = dot(in_ref[:, C:], wo_ref[...], NT).astype(bf16)
        for i in range(2):
            dmix[i] = d_mixed[:, i * HALF : (i + 1) * HALF]

    q, k, v = qkv[g], qkv[2 + g], qkv[4 + g]
    total, sums = attend_heads(range(4), q, k, v, exq[...], exk[...], e_s)
    mixed = total / sums
    mixed_s[g] = mixed.astype(bf16)
    d_own, extra = delta_parts(dmix[g].astype(f32), mixed, sums)
    d_q = attend_back_heads(
        range(4), e_s, q.astype(f32).T.astype(bf16), k, v, d_own.astype(bf16), d_own.T.astype(bf16), extra, dk, dv, g * HALF
    )
    dq[g] = d_q.astype(bf16)

    @pl.when(g == 1)
    def _():
        x = in_ref[:, :C].astype(f32)
        y = x
        for i in range(2):
            y = y + dot(mixed_s[i], wo_ref[i * HALF : (i + 1) * HALF, :], NN)
        out_ref[:, C:] = jnp.where(valid(), y, 0.0).astype(bf16)
        out_ref[:, :C] = input_grad(x, gain_ref[1:2, :], wq_ref, dq, dk, dv, in_ref[:, C:]).astype(bf16)


def far_grads_kernel(in_ref, gain_ref, mixed_ref, dq, dk, dv, pay_ref):
    def put(col, piece):
        pay_ref[:, col : col + piece.shape[1]] = piece.astype(bf16)

    for i in range(2):
        pay_ref[i * HALF : (i + 1) * HALF, 768:1024] = dot(mixed_ref[i], in_ref[:, C:], TN).astype(bf16)
    xhat, _ = norm_parts(in_ref[:, :C].astype(f32))
    weight_grads((xhat * gain_ref[1:2, :]).astype(bf16), dq, dk, dv, put)


def near_finish_kernel(in_ref, xp_ref, gain_ref, wq_ref, dq, dk, dv, dx_ref, res_ref, tmp):
    merge_into(tmp, lambda rows, cols: in_ref[rows, C + cols.start : C + cols.stop].astype(f32), res_ref)
    dx = input_grad(xp_ref[...].astype(f32), gain_ref[0:1, :], wq_ref, dq, dk, dv, in_ref[:, :C])
    merge_into(tmp, lambda rows, cols: dx[rows, cols], dx_ref)


def near_backward_kernel(
    core_ref,
    in_ref,
    normed_ref,
    wo_ref,
    qkv_ref,
    mixed_ref,
    sums_ref,
    two_ref,
    e_ref,
    keep_ref,
    send_ref,
    dq,
    dk,
    dv,
    pay_ref,
    down,
    down_t,
    q_t,
    extra_s,
    acc,
    e_s,
    sem,
):
    step = pl.program_id(0)

    def put(col, piece):
        pay_ref[:, col : col + piece.shape[1]] = piece.astype(bf16)

    def fetch(i):
        slot = i & 1
        cols = pl.ds(pl.multiple_of(i * 2 * WIN, 2 * WIN), 2 * WIN)
        return pltpu.make_async_copy(e_ref.at[:, cols], e_s.at[slot], sem.at[slot])

    @pl.when(step == 0)
    def _():
        fetch(0).start()
        fetch(1).start()
        dy = in_ref[:, :C]
        d_mixed = dot(dy, wo_ref[...], NT).astype(bf16).astype(f32)
        for i in range(2):
            rows = slice(i * HALF, (i + 1) * HALF)
            d_own, extra = delta_parts(d_mixed[:, rows], mixed_ref[i].astype(f32), sums_ref[i])
            down[i] = d_own.astype(bf16)
            down_t[rows, :] = d_own.T.astype(bf16)
            q_t[rows, :] = qkv_ref[i].astype(f32).T.astype(bf16)
            extra_s[i] = extra
            pay_ref[rows, 768:1024] = dot(mixed_ref[i], dy, TN).astype(bf16)
        pay_ref[:, 1024:2048] = two_ref[...]

    fetch(step).wait()
    g = step >> 1
    first = (step & 1) * 2
    base = pl.multiple_of(step * 64, 64)
    d_q = attend_back_heads(
        (first, first + 1),
        e_s.at[step & 1],
        q_t[pl.ds(base, 64), :],
        qkv_ref[2 + g],
        qkv_ref[4 + g],
        down[g],
        down_t[pl.ds(base, 64), :],
        extra_s[g],
        dk,
        dv,
        base,
    )

    @pl.when(step < 2)
    def _():
        fetch(step + 2).start()

    @pl.when(first == 0)
    def _():
        acc[...] = d_q

    @pl.when(first != 0)
    def _():
        dq[g] = (acc[...] + d_q).astype(bf16)

    @pl.when(step == 3)
    def _():
        weight_grads(normed_ref[...], dq, dk, dv, put)
        core = core_ref[0]
        keep_ref[...] = pay_ref[pl.ds(pl.multiple_of(core * HALF, HALF), HALF), :]
        send_ref[...] = pay_ref[pl.ds(pl.multiple_of((1 - core) * HALF, HALF), HALF), :]


def spread_kernel(core_ref, mine_ref, other_ref, gain_ref, wq_ref, gains_ref, qkv_ref, proj_ref):
    core = core_ref[0]
    for ref, half in ((mine_ref, core), (other_ref, 1 - core)):
        rows = pl.ds(pl.multiple_of(half * HALF, HALF), HALF)
        for b in range(2):
            qkv_ref[b, rows, :] = ref[:, b * 1024 : b * 1024 + 768].astype(f32)
            proj_ref[b, rows, :] = ref[:, b * 1024 + 768 : (b + 1) * 1024].astype(f32)
    for b in range(2):
        along = jnp.sum(qkv_ref[b] * wq_ref[b].astype(f32), axis=1, keepdims=True)
        gains_ref[b : b + 1, :] = jnp.broadcast_to(along, (C, HALF)).T[:1] / gain_ref[b : b + 1, :]


def layer(shape, which):
    return pl.BlockSpec((None,) + shape, lambda i: (which, 0, 0))


def spec(shape):
    return pl.BlockSpec(shape, lambda i: (0,) * len(shape))


SCALAR = pl.BlockSpec(memory_space=pltpu.SMEM)
HEAD_PAIR = pl.BlockSpec((WIN, 2 * WIN), lambda i: (0, i))
PARAMS = pltpu.CompilerParams(vmem_limit_bytes=LIMIT)
ROWS = (WIN, C)
PAIR_ROWS = (WIN, 2 * C)
SPLIT_ROWS = (2, WIN, HALF)


def sds(shape, dtype):
    return jax.ShapeDtypeStruct(shape, dtype)


def cost(products):
    return pl.CostEstimate(flops=products * HEADS * 2 * WIN * WIN * HALF, bytes_accessed=2**24, transcendentals=2**23)


def near_forward(n, x, cot, gain, wq, wo):
    return pl.pallas_call(
        near_forward_kernel,
        grid=(4,),
        in_specs=[SCALAR, spec(ROWS), spec(ROWS), spec((2, C)), layer((C, 3 * C), 0), layer((C, C), 0)],
        out_specs=[spec(PAIR_ROWS), spec(ROWS), spec(ROWS), spec((6, WIN, HALF)), spec(SPLIT_ROWS), spec(SPLIT_ROWS), HEAD_PAIR],
        out_shape=[
            sds(PAIR_ROWS, bf16),
            sds(ROWS, bf16),
            sds(ROWS, bf16),
            sds((6, WIN, HALF), bf16),
            sds(SPLIT_ROWS, bf16),
            sds(SPLIT_ROWS, f32),
            sds((WIN, HEADS * WIN), bf16),
        ],
        scratch_shapes=[
            pltpu.VMEM(SPLIT_ROWS, f32),
            pltpu.VMEM((2, WIN, C), f32),
            pltpu.VMEM((WIN, HALF), bf16),
            pltpu.VMEM((WIN, HALF), bf16),
        ],
        compiler_params=PARAMS,
        cost_estimate=cost(2),
        name="near_forward",
    )(n, x, cot, gain, wq, wo)


D_ROWS = [SPLIT_ROWS, (C, WIN), (C, WIN)]
D_SHAPES = [sds(shape, bf16) for shape in D_ROWS]
D_SPECS = [spec(shape) for shape in D_ROWS]


def far_both(n, rows, gain, wq, wo):
    return pl.pallas_call(
        far_kernel,
        grid=(2,),
        in_specs=[SCALAR, spec(PAIR_ROWS), spec((2, C)), layer((C, 3 * C), 1), layer((C, C), 1)],
        out_specs=[spec(PAIR_ROWS), spec(SPLIT_ROWS), *D_SPECS],
        out_shape=[sds(PAIR_ROWS, bf16), sds(SPLIT_ROWS, bf16), *D_SHAPES],
        scratch_shapes=[
            pltpu.VMEM((6, WIN, HALF), bf16),
            pltpu.VMEM(SPLIT_ROWS, bf16),
            pltpu.VMEM((WIN, 4 * WIN), bf16),
            pltpu.VMEM((WIN, HALF), bf16),
            pltpu.VMEM((WIN, HALF), bf16),
        ],
        compiler_params=PARAMS,
        cost_estimate=cost(6),
        name="far_both",
    )(n, rows, gain, wq, wo)


def far_grads(rows, gain, mixed, dq, dk, dv):
    return pl.pallas_call(
        far_grads_kernel,
        grid=(1,),
        in_specs=[spec(PAIR_ROWS), spec((2, C)), spec(SPLIT_ROWS), *D_SPECS],
        out_specs=spec((C, 1024)),
        out_shape=sds((C, 1024), bf16),
        compiler_params=PARAMS,
        cost_estimate=pl.CostEstimate(flops=2**30, bytes_accessed=2**22, transcendentals=0),
        name="far_grads",
    )(rows, gain, mixed, dq, dk, dv)


def near_finish(rows, xp, gain, wq, dq, dk, dv):
    return pl.pallas_call(
        near_finish_kernel,
        grid=(1,),
        in_specs=[spec(PAIR_ROWS), spec(ROWS), spec((2, C)), layer((C, 3 * C), 0), *D_SPECS],
        out_specs=[spec(ROWS), spec(ROWS)],
        out_shape=[sds(ROWS, bf16), sds(ROWS, bf16)],
        scratch_shapes=[pltpu.VMEM(SPLIT_ROWS, f32)],
        compiler_params=PARAMS,
        cost_estimate=pl.CostEstimate(flops=2**30, bytes_accessed=2**22, transcendentals=0),
        name="near_finish",
    )(rows, xp, gain, wq, dq, dk, dv)


def near_backward(core, rows, normed, wo, qkv, mixed, sums, two, e):
    return pl.pallas_call(
        near_backward_kernel,
        grid=(4,),
        in_specs=[
            SCALAR,
            spec(PAIR_ROWS),
            spec(ROWS),
            layer((C, C), 0),
            spec((6, WIN, HALF)),
            spec(SPLIT_ROWS),
            spec(SPLIT_ROWS),
            spec((C, 1024)),
            pl.BlockSpec(memory_space=pl.ANY),
        ],
        out_specs=[spec((HALF, 2048)), spec((HALF, 2048)), *D_SPECS],
        out_shape=[sds((HALF, 2048), bf16), sds((HALF, 2048), bf16), *D_SHAPES],
        scratch_shapes=[
            pltpu.VMEM((C, 2048), bf16),
            pltpu.VMEM(SPLIT_ROWS, bf16),
            pltpu.VMEM((C, WIN), bf16),
            pltpu.VMEM((C, WIN), bf16),
            pltpu.VMEM(SPLIT_ROWS, bf16),
            pltpu.VMEM((WIN, HALF), f32),
            pltpu.VMEM((2, WIN, 2 * WIN), bf16),
            pltpu.SemaphoreType.DMA((2,)),
        ],
        compiler_params=PARAMS,
        cost_estimate=cost(4),
        name="near_backward",
    )(core, rows, normed, wo, qkv, mixed, sums, two, e)


def spread(core, mine, other, gain, wq):
    vmem = pl.BlockSpec(memory_space=pltpu.VMEM)
    return pl.pallas_call(
        spread_kernel,
        in_specs=[SCALAR, vmem, vmem, vmem, vmem],
        out_shape=[sds((2, C), f32), sds((2, C, 3 * C), f32), sds((2, C, C), f32)],
        compiler_params=PARAMS,
        name="spread",
    )(core, mine, other, gain, wq)


def exchange(rows, axis, groups=None):
    return lax.all_to_all(rows, axis, split_axis=0, concat_axis=0, tiled=True, axis_index_groups=groups)


def sum_everywhere(keep, send, factor, beside):
    scenes, groups = lax.axis_size("scene"), lax.axis_size("seq")
    width = keep.shape[1]
    pair = [(i, i ^ 1) for i in range(groups)]
    chips = [list(range(core, groups, 2)) for core in range(2)]
    many = groups // 2
    part = (keep.astype(f32) + lax.ppermute(send, "seq", pair).astype(f32)).astype(bf16)
    part = exchange(part.reshape(many, scenes, width), "seq", chips)
    part, beside = lax.optimization_barrier((part, beside))
    part = jnp.sum(part.astype(f32), axis=0)
    part = exchange(part.astype(bf16).reshape(scenes, 1, width), "scene").astype(f32)
    row = (jnp.sum(part, axis=0, keepdims=True) * factor).astype(bf16)
    rows = exchange(jnp.broadcast_to(row, (scenes, 1, width)), "scene").reshape(1, scenes, width)
    mine = exchange(jnp.broadcast_to(rows, (many, scenes, width)), "seq", chips).reshape(HALF, width)
    return mine, lax.ppermute(mine, "seq", pair), beside


def body(x_in, counts, ln_gains, w_qkv, w_proj, cotangent):
    groups = lax.axis_size("seq")
    place = lax.axis_index("seq")
    factor = (WIN * lax.axis_size("scene") * groups) ** (-0.5)
    n_near = counts - place * WIN
    n_far = (counts - place + groups - 1) // groups

    def swap(rows):
        return exchange(rows.reshape(SPLIT, PIECE, 2 * C), "seq").reshape(PAIR_ROWS)

    core = jnp.full((1,), place % 2, jnp.int32)
    first, xp, normed, qkv, mixed, sums, e = near_forward(n_near, x_in, cotangent, ln_gains, w_qkv, w_proj)
    rows_far = swap(first)
    back, *far_parts = far_both(n_far, rows_far, ln_gains, w_qkv, w_proj)
    rows = swap(back)
    two = far_grads(rows_far, ln_gains, *far_parts)
    keep, send, *d_rows = near_backward(core, rows, normed, w_proj, qkv, mixed, sums, two, e)
    beside = near_finish(rows, xp, ln_gains, w_qkv, *d_rows)
    mine, other, (d_input, result) = sum_everywhere(keep, send, factor, tuple(beside))
    gains, grads, projs = spread(core, mine, other, ln_gains, w_qkv)
    return result, d_input, gains, grads, projs


def solution(mesh):
    in_specs = (P(("scene", "seq"), None), P("scene"), P(), P(), P(), P(("scene", "seq"), None))
    out_specs = (P(("scene", "seq"), None), P(("scene", "seq"), None), P(), P(), P())
    return jax.shard_map(body, mesh=mesh, in_specs=in_specs, out_specs=out_specs, check_vma=False)
```

time: 208 us -> 199 us (0.957)
  blocking collectives: 53.7 us -> 41.4 us
  starting transfers between devices: 17 us -> 20.5 us
    all_to_all x4 -> x3, blocking collectives: 53.7 us -> 41.4 us  [exchange(): lax.all_to_all(rows, axis, split_axis=0, concat_axis=0, tiled=True, axis_...]
    pallas_call x1 -> x3, Pallas kernels: 2.65 us -> 11.2 us  [the longest x1 4.36 us: near_finish(): pl.pallas_call(near_finish_kernel, grid=(1,), in_specs=[spec(PAIR_ROWS),...]
    pallas_call x1, Pallas kernels: 39.2 us -> 32.5 us  [far_both(): pl.pallas_call(far_kernel, grid=(2,), in_specs=[SCALAR, spec(PAIR_ROWS),...]
    all_to_all x2 -> x3, starting transfers between devices: 11 us -> 14.5 us  [exchange(): lax.all_to_all(rows, axis, split_axis=0, concat_axis=0, tiled=True, axis_...]
    all_to_all x2 -> x3, waiting for transfers between devices: 30.2 us -> 31.1 us  [exchange(): lax.all_to_all(rows, axis, split_axis=0, concat_axis=0, tiled=True, axis_...]
  transfers between devices with their start and end apart: 4 -> 5, of which waited for: 4 -> 5; matrix products, arithmetic and copies ran while one was open for 0% -> 0% of each run, Pallas kernels for 0% -> 4%
where the time goes in v1:
time: 199 us
  Pallas kernels  92.8 us (47%)
  blocking collectives  41.4 us (21%)
  waiting for transfers between devices  34.4 us (17%)
  starting transfers between devices  20.5 us (10%)
  other arithmetic  4.34 us (2%)
  local copies, waits for them, and re-layouts  3.97 us (2%)
    all_to_all x3, blocking collectives, exchange(): lax.all_to_all(rows, axis, split_axis=0, concat_axis=0, tiled=True, axis_...  41.4 us
    pallas_call x1, Pallas kernels, far_both(): pl.pallas_call(far_kernel, grid=(2,), in_specs=[SCALAR, spec(PAIR_ROWS),...  32.5 us
    all_to_all x3, waiting for transfers between devices, exchange(): lax.all_to_all(rows, axis, split_axis=0, concat_axis=0, tiled=True, axis_...  31.1 us
    pallas_call x1, Pallas kernels, near_backward(): pl.pallas_call(near_backward_kernel, grid=(4,), in_specs=[SCALAR, spec(PA...  27.2 us
    pallas_call x1, Pallas kernels, near_forward(): pl.pallas_call(near_forward_kernel, grid=(4,), in_specs=[SCALAR, spec(ROW...  21.9 us
    all_to_all x3, starting transfers between devices, exchange(): lax.all_to_all(rows, axis, split_axis=0, concat_axis=0, tiled=True, axis_...  14.5 us
    ppermute x1, starting transfers between devices, sum_everywhere(): return (mine, lax.ppermute(mine, 'seq', pair), beside)  5.05 us
    pallas_call x1, Pallas kernels, near_finish(): pl.pallas_call(near_finish_kernel, grid=(1,), in_specs=[spec(PAIR_ROWS),...  4.36 us
  transfers between devices with their start and end apart: 5, of which 5 were waited for; matrix products, arithmetic and copies ran while one was open for 0% of the time, Pallas kernels for 4%

profile of v1, /device:TPU:1, one launch (start us, length us, event | category | flops | bytes accessed | tf_op | source)
XLA Modules:
  0.0 198.8 jit_solution(5798587976371721248)
XLA Ops:
  1.3 21.9 %near_forward.1 = (bf16[1024,512]{1,0:T(8,128)(2,1)}, bf16[1024,256]{1,0:T(8,128)(2,1)}, bf16[1024,256]{1,0:T(8,128)(2,1)}, bf16[6,1024,128]{2,1,0:T(8,128)(2,1)...) custom-call(s32[1]{0:T(128)S(6)} %sub.24.n_ref, bf16[1024,256]{1,0:T(8,128)(2,1)} %x_ref.1, ...), custom_call_target="tpu_custom_call" | custom-call | flops 4294967296 | bytes 16777216 | tf_op jit(solution)/shard_map/near_forward/pallas_call | solution.py:383
  23.2 6.7 %all-to-all-start = ((bf16[8,128,512]{2,1,0:T(8,128)(2,1)}), bf16[8,128,512]{2,1,0:T(8,128)(2,1)S(1)}, u32[]{:S(2)}, u32[]{:S(2)}) async-start(bf16[8,128,512]{2,1,0:T(8,128)(2,1)} %bitcast.19), calls=%async_computation | async-start | bytes 2097152 | tf_op jit(solution)/shard_map/all_to_all | solution.py:506
  29.9 15.1 %all-to-all-done = bf16[8,128,512]{2,1,0:T(8,128)(2,1)S(1)} async-done(((bf16[8,128,512]{2,1,0:T(8,128)(2,1)}), bf16[8,128,512]{2,1,0:T(8,128)(2,1)S(1)}, u32[]{:S(2)}, u32[]{:S(2)}) %all-to-all-start) | async-done | bytes 1048608 | tf_op jit(solution)/shard_map/all_to_all | solution.py:506
  45.0 0.0 copy-start.1
  45.0 1.0 copy-done.1
  46.0 32.5 %far_both.1 = (bf16[1024,512]{1,0:T(8,128)(2,1)}, bf16[2,1024,128]{2,1,0:T(8,128)(2,1)}, bf16[2,1024,128]{2,1,0:T(8,128)(2,1)}, bf16[256,1024]{1,0:T(8,128)(2,1)}, bf16[256,1024]{1,0:T(8,128)(2,1)}) custom-call(s32[1]{0:T(128)S(6)} %select_n.13.n_ref, bf16[1024,512]{1,0:T(8,128)(2,1)} %bitcast.15, f32[2,256]{1,0:T(2,128)} %gain_ref.9, ...), custom_call_target="tpu_custom_call" | custom-call | flops 12884901888 | bytes 16777216 | tf_op jit(solution)/shard_map/far_both/pallas_call | solution.py:415
  78.5 4.3 %all-to-all-start.1 = ((bf16[8,128,512]{2,1,0:T(8,128)(2,1)}), bf16[8,128,512]{2,1,0:T(8,128)(2,1)S(1)}, u32[]{:S(2)}, u32[]{:S(2)}) async-start(bf16[8,128,512]{2,1,0:T(8,128)(2,1)} %bitcast.20), calls=%async_computation.1 | async-start | bytes 2097152 | tf_op jit(solution)/shard_map/all_to_all | solution.py:506
  82.9 4.0 %far_grads.1.two_ref = bf16[256,1024]{1,0:T(8,128)(2,1)} custom-call(bf16[1024,512]{1,0:T(8,128)(2,1)} %bitcast.16, f32[2,256]{1,0:T(2,128)} %gain_ref.9, bf16[2,1024,128]{2,1,0:T(8,128)(2,1)} %get-tuple-element.36.mixed_ref, bf16[2,1024,128]{2,1,0:T(8,128)(2,1)} %get-tuple-element.37.dq, bf16[256,1024]{1,0:T(8,128)(2,1)} %get-tuple-element.38.dk, ...), custom_call_target="tpu_custom_call" | custom-call | flops 1073741824 | bytes 4194304 | tf_op jit(solution)/shard_map/far_grads/pallas_call | solution.py:435
  86.8 11.1 %all-to-all-done.1 = bf16[8,128,512]{2,1,0:T(8,128)(2,1)S(1)} async-done(((bf16[8,128,512]{2,1,0:T(8,128)(2,1)}), bf16[8,128,512]{2,1,0:T(8,128)(2,1)S(1)}, u32[]{:S(2)}, u32[]{:S(2)}) %all-to-all-start.1) | async-done | bytes 1048608 | tf_op jit(solution)/shard_map/all_to_all | solution.py:506
  98.0 0.0 copy-start.2
  98.0 1.0 copy-done.2
  99.0 27.2 %near_backward.1 = (bf16[128,2048]{1,0:T(8,128)(2,1)}, bf16[128,2048]{1,0:T(8,128)(2,1)}, bf16[2,1024,128]{2,1,0:T(8,128)(2,1)}, bf16[256,1024]{1,0:T(8,128)(2,1)}, bf16[256,1024]{1,0:T(8,128)(2,1)}) custom-call(s32[1]{0:T(128)} %bitcast.core_ref, bf16[1024,512]{1,0:T(8,128)(2,1)} %bitcast.17, bf16[1024,256]{1,0:T(8,128)(2,1)} %get-tuple-element.32.normed_ref, ...), custom_call_target="tpu_custom_call" | custom-call | flops 8589934592 | bytes 16777216 | tf_op jit(solution)/shard_map/near_backward/pallas_call | solution.py:462
  126.2 1.0 collective-permute-start
  127.2 1.7 collective-permute-done
  128.9 2.0 add_convert_fusion
  130.9 3.5 %all-to-all-start.2 = ((bf16[4,32,2048]{2,1,0:T(8,128)(2,1)}), bf16[4,32,2048]{2,1,0:T(8,128)(2,1)S(1)}, u32[]{:S(2)}, u32[]{:S(2)}) async-start(bf16[4,32,2048]{2,1,0:T(8,128)(2,1)} %bitcast.7), calls=%async_computation.2 | async-start | bytes 1048576 | tf_op jit(solution)/shard_map/all_to_all | solution.py:506
  134.4 4.4 %near_finish.1 = (bf16[1024,256]{1,0:T(8,128)(2,1)}, bf16[1024,256]{1,0:T(8,128)(2,1)}) custom-call(bf16[1024,512]{1,0:T(8,128)(2,1)} %bitcast.18, bf16[1024,256]{1,0:T(8,128)(2,1)} %get-tuple-element.43.xp_ref, f32[2,256]{1,0:T(2,128)} %gain_ref.9, bf16[2,256,768]{2,1,0:T(8,128)(2,1)} %wq_ref.7, bf16[2,1024,128]{2,1,0:T(8,128)(2,1)} %get-tuple-element.44.dq, ...), custom_call_target="tpu_custom_call" | custom-call | flops 1073741824 | bytes 4194304 | tf_op jit(solution)/shard_map/near_finish/pallas_call | solution.py:448
  138.7 4.8 %all-to-all-done.2 = bf16[4,32,2048]{2,1,0:T(8,128)(2,1)S(1)} async-done(((bf16[4,32,2048]{2,1,0:T(8,128)(2,1)}), bf16[4,32,2048]{2,1,0:T(8,128)(2,1)S(1)}, u32[]{:S(2)}, u32[]{:S(2)}) %all-to-all-start.2) | async-done | bytes 524320 | tf_op jit(solution)/shard_map/all_to_all | solution.py:506
  143.6 0.1 reduce_sum.21
  143.6 0.5 broadcast.11
  144.2 0.7 reduce.2
  144.8 0.1 reshape.55
  144.9 19.4 %all_to_all.30 = bf16[32,2,1024]{2,1,0:T(2,128)(2,1)S(1)} all-to-all(bf16[32,2,1024]{2,1,0:T(2,128)(2,1)S(1)} %reshape.55), channel_id=1, replica_groups=mesh['scene'=32,'seq'=8] {'scene'}, dimensions={0} | all-to-all | bytes 262144 | tf_op jit(solution)/shard_map/all_to_all | solution.py:506
  164.4 0.1 reshape.56
  164.5 0.2 convert_reduce_fusion
  164.7 0.1 broadcast_in_dim.17
  164.9 1.4 reduce.3
  166.2 0.1 reshape.57
  166.3 12.6 %all_to_all.31 = bf16[32,2,1024]{2,1,0:T(2,128)(2,1)S(1)} all-to-all(bf16[32,2,1024]{2,1,0:T(2,128)(2,1)S(1)} %reshape.57), channel_id=1, replica_groups=mesh['scene'=32,'seq'=8] {'scene'}, dimensions={0} | all-to-all | bytes 262144 | tf_op jit(solution)/shard_map/all_to_all | solution.py:506
  179.0 0.1 reshape.58
  179.1 0.1 copy.14
  179.2 9.3 %all_to_all.32 = bf16[4,32,2048]{2,1,0:T(8,128)(2,1)S(1)} all-to-all(bf16[4,32,2048]{2,1,0:T(8,128)(2,1)S(1)} %broadcast_in_dim.19), channel_id=1, replica_groups={{0,2,4,6},{1,3,5,7},{8,10,12,14},{9,11,13,15},{16,18,20,22},{17,19,21,2..., dimensions={0} | all-to-all | bytes 1048576 | tf_op jit(solution)/shard_map/all_to_all | solution.py:506
  188.6 0.0 copy-start
  188.6 5.1 %collective-permute-start.1 = (bf16[128,2048]{1,0:T(8,128)(2,1)S(1)}, bf16[128,2048]{1,0:T(8,128)(2,1)S(1)}, u32[]{:S(2)}, u32[]{:S(2)}) collective-permute-start(bf16[128,2048]{1,0:T(8,128)(2,1)S(1)} %bitcast.13), channel_id=1, source_target_pairs={{0,1},{1,0},{2,3},{3,2},{4,5},{5,4},{6,7},{7,6},{8,9},{9,8},{10,11... | collective-permute-start | bytes 1572872 | tf_op jit(solution)/shard_map/ppermute | solution.py:523
  193.6 1.5 collective-permute-done.1.other_ref
  195.1 0.0 copy-done
  195.1 0.0 copy-start.3
  195.1 0.8 copy-done.3
  195.9 2.9 %spread.1 = (f32[2,256]{1,0:T(2,128)}, f32[2,256,768]{2,1,0:T(8,128)}, f32[2,256,256]{2,1,0:T(8,128)}) custom-call(s32[1]{0:T(128)} %bitcast.core_ref, bf16[128,2048]{1,0:T(8,128)(2,1)} %bitcast.14, bf16[128,2048]{1,0:T(8,128)(2,1)} %copy-done.3, f32[2,256]{1,0:T(2,128)} %gain_ref.9, bf16[2,256,768]{2,1,0:T(8,128)(2,1)} %wq_ref.7), custom_call_target="tpu_custom_call" | custom-call | tf_op jit(solution)/shard_map/spread/pallas_call | solution.py:496
  (2 shorter events, 0.1 us)
Async XLA Ops:
  23.2 21.8 %all-to-all-start = ((bf16[8,128,512]{2,1,0:T(8,128)(2,1)}), bf16[8,128,512]{2,1,0:T(8,128)(2,1)S(1)}, u32[]{:S(2)}, u32[]{:S(2)}) async-start(bf16[8,128,512]{2,1,0:T(8,128)(2,1)} %bitcast.19), calls=%async_computation | async-start | bytes 2097152 | tf_op jit(solution)/shard_map/all_to_all | solution.py:506
  45.0 1.0 copy-start.1
  78.5 19.4 %all-to-all-start.1 = ((bf16[8,128,512]{2,1,0:T(8,128)(2,1)}), bf16[8,128,512]{2,1,0:T(8,128)(2,1)S(1)}, u32[]{:S(2)}, u32[]{:S(2)}) async-start(bf16[8,128,512]{2,1,0:T(8,128)(2,1)} %bitcast.20), calls=%async_computation.1 | async-start | bytes 2097152 | tf_op jit(solution)/shard_map/all_to_all | solution.py:506
  98.0 1.0 copy-start.2
  126.2 2.7 %collective-permute-start = (bf16[128,2048]{1,0:T(8,128)(2,1)}, bf16[128,2048]{1,0:T(8,128)(2,1)S(1)}, u32[]{:S(2)}, u32[]{:S(2)}) collective-permute-start(bf16[128,2048]{1,0:T(8,128)(2,1)} %get-tuple-element.42), channel_id=1, source_target_pairs={{0,1},{1,0},{2,3},{3,2},{4,5},{5,4},{6,7},{7,6},{8,9},{9,8},{10,11... | collective-permute-start | bytes 1572872 | tf_op jit(solution)/shard_map/ppermute | solution.py:515
  130.9 12.7 %all-to-all-start.2 = ((bf16[4,32,2048]{2,1,0:T(8,128)(2,1)}), bf16[4,32,2048]{2,1,0:T(8,128)(2,1)S(1)}, u32[]{:S(2)}, u32[]{:S(2)}) async-start(bf16[4,32,2048]{2,1,0:T(8,128)(2,1)} %bitcast.7), calls=%async_computation.2 | async-start | bytes 1048576 | tf_op jit(solution)/shard_map/all_to_all | solution.py:506
  188.6 6.6 %copy-start = (bf16[4,32,2048]{2,1,0:T(8,128)(2,1)}, bf16[4,32,2048]{2,1,0:T(8,128)(2,1)S(1)}, u32[]{:S(2)}) copy-start(bf16[4,32,2048]{2,1,0:T(8,128)(2,1)S(1)} %all_to_all.32) | copy-start | bytes 1572868
  188.6 6.6 %collective-permute-start.1 = (bf16[128,2048]{1,0:T(8,128)(2,1)S(1)}, bf16[128,2048]{1,0:T(8,128)(2,1)S(1)}, u32[]{:S(2)}, u32[]{:S(2)}) collective-permute-start(bf16[128,2048]{1,0:T(8,128)(2,1)S(1)} %bitcast.13), channel_id=1, source_target_pairs={{0,1},{1,0},{2,3},{3,2},{4,5},{5,4},{6,7},{7,6},{8,9},{9,8},{10,11... | collective-permute-start | bytes 1572872 | tf_op jit(solution)/shard_map/ppermute | solution.py:523
  195.1 0.8 copy-start.3
